TPU v7x, 32 devices: a whole 2x2x4 slice. The times are simulated.
32 devices in a mesh: grp: 2 (over x), sec: 8 (over z, y), head: 2 (over core).
Axes of the slice: x: 2, y: 2, z: 4, core: 2. Of those that a mesh axis runs over, the one named last changes fastest.
Arguments:
- patches: bfloat16 [4, 64, 1408], P('grp', 'head'), parts along dimension 0, may hold values from -6 to 6
- stale_kv: bfloat16 [16, 2, 512, 1408], P(('grp', 'sec'), None, None, 'head'), parts along dimension 0, as said below
- qkv_weight: bfloat16 [8, 3, 1408, 1408], P('sec', None, None, 'head'), may hold values from -0.15625 to 0.15625
- out_weight: bfloat16 [8, 1408, 1408], P('sec', 'head'), may hold values from -0.15625 to 0.15625
- skip_joined_weight: bfloat16 [8, 2816, 1408], P('sec'), may hold values from -0.109375 to 0.109375
- qk_gain: bfloat16 [8, 2, 1408], P('sec', None, 'head'), may hold values from 0.5 to 1.5
- order: int32 [16], P('grp'), parts along dimension 0, may hold values from 0 to 7, each once
- tile_index: int32 [2], P('grp'), parts along dimension 0, may hold values from 0 to 15
Outputs:
- section_out: bfloat16 [8, 4, 64, 1408], P('sec', 'grp', 'head'), parts along dimension 1
There are 2 independent parts, one for each index of `grp`. A program takes and returns all parts, laid end to end along the dimension named above; an argument that names none is the same for every part. Nothing has to cross between parts.
Inputs may be any that keep to these rules, and one draw needn't show every extreme that they name: The first 2 entries name the slots of the patches, in the order of patches; all entries are distinct. `stale_kv`: in the key half, the 88 entries of each head of each row have a root mean square of at most 1.51.
All inputs are finite; a program needn't handle non-finite values.
Results may differ from a plain program's by a relative error of at most 0.018.
Values may be sent and summed in bfloat16 or wider, within the bound.
A program may use at most 64 MiB of HBM per device.

v0:
```python
import math

import jax
import jax.numpy as jnp
from jax import lax
from jax.sharding import PartitionSpec as P

HEAD_DIM = 88


EPSILON = 1e-06


def shifted(value, axis, steps):
    count = lax.axis_size(axis)
    leading, last = (max(0, -steps), min(count, count - steps))
    return lax.ppermute(value, axis, [(source, source + steps) for source in range(leading, last)])


def layer_norm(tensor):
    average = jnp.mean(tensor, axis=-1, keepdims=True)
    centred = tensor - average
    variance = jnp.mean(centred * centred, axis=-1, keepdims=True)
    return centred / jnp.sqrt(variance + EPSILON)


def rotate(tensor, position):
    half_width = tensor.shape[-1] // 2
    inverse = 10000.0 ** (-jnp.arange(half_width, dtype=jnp.float32) / half_width)
    angles = position[:, None] * inverse[None, :]
    cos_table = jnp.cos(angles)[:, None, :]
    sin_table = jnp.sin(angles)[:, None, :]
    leading = tensor[..., :half_width]
    trailing_half = tensor[..., half_width:]
    return jnp.concatenate(
        [
            leading * cos_table - trailing_half * sin_table,
            leading * sin_table + trailing_half * cos_table,
        ],
        axis=-1,
    )


def head_norm(projected, gain, position):
    row_count = projected.shape[0]
    heads_here = projected.shape[-1] // HEAD_DIM
    shaped = projected.reshape(row_count, heads_here, HEAD_DIM)
    scaled = layer_norm(shaped) * gain.reshape(heads_here, HEAD_DIM)
    return rotate(scaled, position).reshape(row_count, heads_here * HEAD_DIM).astype(jnp.bfloat16)


def attention_result(query_rot, key_cache, value_cache):
    row_count = query_rot.shape[0]
    heads_here = query_rot.shape[1] // HEAD_DIM
    query = query_rot.reshape(row_count, heads_here, HEAD_DIM)
    key_heads = key_cache.reshape(key_cache.shape[0], heads_here, HEAD_DIM)
    value_heads = value_cache.reshape(value_cache.shape[0], heads_here, HEAD_DIM)
    scores = jnp.einsum(
        "qhd,khd->hqk", query, key_heads, preferred_element_type=jnp.float32
    ) / math.sqrt(HEAD_DIM)
    expd = jnp.exp(scores)
    weights = (expd / jnp.sum(expd, axis=-1, keepdims=True)).astype(jnp.bfloat16)
    mixed = jnp.einsum("hqk,khd->qhd", weights, value_heads, preferred_element_type=jnp.float32)
    return mixed.reshape(row_count, heads_here * HEAD_DIM).astype(jnp.bfloat16)


def body(patches, stale_kv, qkv_weight, out_weight, skip_joined_weight, qk_gain, order, tile_index):
    patch_count = patches.shape[0]
    own_rows = patches.shape[1]
    model_width = patches.shape[2]
    patch_rows = own_rows * lax.axis_size("head")
    tile_rows = stale_kv.shape[2]
    sections = lax.axis_size("sec")
    half_count = sections // 2
    section = lax.axis_index("sec")
    decoder = section >= half_count
    partner = sections - 1 - section
    section_ids = jnp.arange(sections, dtype=jnp.int32)
    sources = jnp.where(section_ids >= half_count, sections - 1 - section_ids, 0)
    gain_pair = qk_gain[0].astype(jnp.float32)
    weights_qkv = qkv_weight[0]
    w_skip = skip_joined_weight[0]
    offsets = jnp.arange(patch_rows, dtype=jnp.int32)
    piece_rows = own_rows // sections
    w_out = lax.all_gather(out_weight[0], "head", axis=0, tiled=True)

    def run_segment(moment, carried, route):
        incoming, key_cache, value_cache, skip_cache, finished = carried
        patch_idx = moment - section
        active_patch = (patch_idx >= 0) & (patch_idx < patch_count)
        which_patch = jnp.clip(patch_idx, 0, patch_count - 1)
        source = jnp.where(section == 0, patches[which_patch], incoming)
        skip_row = lax.dynamic_index_in_dim(skip_cache, which_patch, 0, keepdims=False)

        def with_skip(operands):
            anchor, skip_in = operands
            joined = jnp.concatenate([anchor, skip_in], axis=1)
            mixed = jnp.dot(joined, w_skip, preferred_element_type=jnp.float32)
            return layer_norm(mixed).astype(jnp.bfloat16)

        def without(operands):
            return operands[0]

        residual = lax.cond(decoder & active_patch, with_skip, without, (source, skip_row))
        normed = layer_norm(residual.astype(jnp.float32)).astype(jnp.bfloat16)
        rows_all = lax.all_gather(normed, "head", axis=0, tiled=True)
        row_start = order[which_patch] * patch_rows
        position = (tile_index[0] * tile_rows + row_start + offsets).astype(jnp.float32)

        def project(operands):
            rows_in, key_buf, value_buf = operands
            projected = jnp.einsum(
                "rd,cde->cre", rows_in, weights_qkv, preferred_element_type=jnp.float32
            )
            query_rot = head_norm(projected[0], gain_pair[0], position)
            key_rot = head_norm(projected[1], gain_pair[1], position)
            value_new = projected[2].astype(jnp.bfloat16)
            key_buf = lax.dynamic_update_slice_in_dim(key_buf, key_rot, row_start, 0)
            value_buf = lax.dynamic_update_slice_in_dim(value_buf, value_new, row_start, 0)
            return (attention_result(query_rot, key_buf, value_buf), key_buf, value_buf)

        def resting_patches(operands):
            rows_in, key_buf, value_buf = operands
            return (jnp.zeros((patch_rows, key_buf.shape[1]), jnp.bfloat16), key_buf, value_buf)

        attended, key_cache, value_cache = lax.cond(
            active_patch, project, resting_patches, (rows_all, key_cache, value_cache)
        )
        regrouped = lax.all_to_all(attended, "head", split_axis=0, concat_axis=1, tiled=True)
        update = jnp.dot(regrouped, w_out, preferred_element_type=jnp.float32)
        produced = (residual.astype(jnp.float32) + update).astype(jnp.bfloat16)
        earlier = lax.dynamic_index_in_dim(finished, which_patch, 0, keepdims=False)
        finished = lax.dynamic_update_index_in_dim(
            finished, jnp.where(active_patch, produced, earlier), which_patch, 0
        )
        if route:
            scattered = lax.all_to_all(produced, "sec", split_axis=0, concat_axis=0, tiled=True)
            pieces = scattered.reshape(sections, piece_rows, model_width)
            chosen = jnp.take(pieces, sources, axis=0).reshape(own_rows, model_width)
            arrived = lax.all_to_all(chosen, "sec", split_axis=0, concat_axis=0, tiled=True)
            lag_patch = moment - partner
            usable = decoder & (lag_patch >= 0) & (lag_patch < patch_count)
            lag_clip = jnp.clip(lag_patch, 0, patch_count - 1)
            previous = lax.dynamic_index_in_dim(skip_cache, lag_clip, 0, keepdims=False)
            skip_cache = lax.dynamic_update_index_in_dim(
                skip_cache, jnp.where(usable, arrived, previous), lag_clip, 0
            )
        incoming = shifted(produced, "sec", 1)
        return (incoming, key_cache, value_cache, skip_cache, finished)

    def routed_segment(moment, carried):
        return run_segment(moment, carried, True)

    def plain_segment(moment, carried):
        return run_segment(moment, carried, False)

    carried = (
        jnp.zeros((own_rows, model_width), jnp.bfloat16),
        stale_kv[0, 0],
        stale_kv[0, 1],
        jnp.zeros((patch_count, own_rows, model_width), jnp.bfloat16),
        jnp.zeros((patch_count, own_rows, model_width), jnp.bfloat16),
    )
    route_end = half_count + patch_count - 1
    carried = lax.fori_loop(0, route_end, routed_segment, carried)
    carried = lax.fori_loop(route_end, sections + patch_count - 1, plain_segment, carried)
    return carried[4][None]


def solution(mesh):
    return jax.shard_map(
        body,
        mesh=mesh,
        in_specs=(
            P("grp", "head", None),
            P(("grp", "sec"), None, None, "head"),
            P("sec", None, None, "head"),
            P("sec", "head", None),
            P("sec", None, None),
            P("sec", None, "head"),
            P("grp"),
            P("grp"),
        ),
        out_specs=P("sec", "grp", "head", None),
        check_vma=False,
    )
```

profile of v0, /device:TPU:29, one launch (start us, length us, event | category | flops | bytes accessed | tf_op | source)
XLA Modules:
  0.0 454.7 jit_solution(7727697982292966009)
XLA Ops:
  10.9 13.1 %all-gather.3.cloned.1.call-done = bf16[1,1408,1408]{2,1,0:T(8,128)(2,1)} async-done(((bf16[1,704,1408]{2,1,0:T(8,128)(2,1)}), bf16[1,1408,1408]{2,1,0:T(8,128)(2,1)}) %all-gather.3.cloned.1.call-update) | async-done | bytes 3964944 | tf_op jit(solution)/shard_map/all_gather | solution.py:85
  24.0 261.3 %while.48 = (s32[]{:T(128)}, bf16[32,1408]{1,0:T(8,128)(2,1)S(1)}, bf16[512,704]{0,1:T(8,128)(2,1)S(1)}, bf16[512,704]{0,1:T(8,128)(2,1)}, bf16[2,32,1408]{2,1,0...) while((s32[]{:T(128)}, bf16[32,1408]{1,0:T(8,128)(2,1)S(1)}, ...), condition=%wide.region_15.16_spmd.clone.clone, body=%wide.region_0.15_spmd.clone.clone.sunk | while | flops 857036992 | bytes 32607800 | solution.py:165
  37.6 19.1 %all-to-all-start.2 = ((bf16[8,4,1408]{2,1,0:T(4,128)(2,1)}), bf16[8,4,1408]{2,1,0:T(4,128)(2,1)S(1)}, u32[]{:S(2)}, u32[]{:S(2)}) async-start(bf16[8,4,1408]{2,1,0:T(4,128)(2,1)} %all_to_all.124), calls=%async_computation.2 | async-start | bytes 180224 | tf_op jit(solution)/shard_map/while/body/eval_jaxpr/all_to_all | solution.py:137
  61.4 5.9 %all-to-all-start.3 = ((bf16[8,4,1408]{2,1,0:T(4,128)(2,1)}), bf16[8,4,1408]{2,1,0:T(4,128)(2,1)S(1)}, u32[]{:S(2)}, u32[]{:S(2)}) async-start(bf16[8,4,1408]{2,1,0:T(4,128)(2,1)} %broadcast_select_fusion.2), calls=%async_computation.3 | async-start | bytes 180224 | tf_op jit(solution)/shard_map/while/body/eval_jaxpr/all_to_all | solution.py:140
  88.9 18.6 %all-to-all-start.2 = ((bf16[8,4,1408]{2,1,0:T(4,128)(2,1)}), bf16[8,4,1408]{2,1,0:T(4,128)(2,1)S(1)}, u32[]{:S(2)}, u32[]{:S(2)}) async-start(bf16[8,4,1408]{2,1,0:T(4,128)(2,1)} %all_to_all.124), calls=%async_computation.2 | async-start | bytes 180224 | tf_op jit(solution)/shard_map/while/body/eval_jaxpr/all_to_all | solution.py:137
  111.3 6.9 %all-to-all-start.3 = ((bf16[8,4,1408]{2,1,0:T(4,128)(2,1)}), bf16[8,4,1408]{2,1,0:T(4,128)(2,1)S(1)}, u32[]{:S(2)}, u32[]{:S(2)}) async-start(bf16[8,4,1408]{2,1,0:T(4,128)(2,1)} %broadcast_select_fusion.2), calls=%async_computation.3 | async-start | bytes 180224 | tf_op jit(solution)/shard_map/while/body/eval_jaxpr/all_to_all | solution.py:140
  124.8 4.8 %all_gather.28 = bf16[64,1408]{1,0:T(8,128)(2,1)S(1)} all-gather(bf16[32,1408]{1,0:T(8,128)(2,1)S(1)} %divide_convert_fusion.11), channel_id=1, replica_groups=mesh['grp'=2,'sec'=8,'head'=2] {'head'}, dimensions={0}, use_global_device_ids=true | all-gather | bytes 270336 | tf_op jit(solution)/shard_map/while/body/eval_jaxpr/all_gather | solution.py:106
  139.9 19.5 %all-to-all-start.2 = ((bf16[8,4,1408]{2,1,0:T(4,128)(2,1)}), bf16[8,4,1408]{2,1,0:T(4,128)(2,1)S(1)}, u32[]{:S(2)}, u32[]{:S(2)}) async-start(bf16[8,4,1408]{2,1,0:T(4,128)(2,1)} %all_to_all.124), calls=%async_computation.2 | async-start | bytes 180224 | tf_op jit(solution)/shard_map/while/body/eval_jaxpr/all_to_all | solution.py:137
  163.9 6.2 %all-to-all-start.3 = ((bf16[8,4,1408]{2,1,0:T(4,128)(2,1)}), bf16[8,4,1408]{2,1,0:T(4,128)(2,1)S(1)}, u32[]{:S(2)}, u32[]{:S(2)}) async-start(bf16[8,4,1408]{2,1,0:T(4,128)(2,1)} %broadcast_select_fusion.2), calls=%async_computation.3 | async-start | bytes 180224 | tf_op jit(solution)/shard_map/while/body/eval_jaxpr/all_to_all | solution.py:140
  176.7 4.8 %all_gather.28 = bf16[64,1408]{1,0:T(8,128)(2,1)S(1)} all-gather(bf16[32,1408]{1,0:T(8,128)(2,1)S(1)} %divide_convert_fusion.11), channel_id=1, replica_groups=mesh['grp'=2,'sec'=8,'head'=2] {'head'}, dimensions={0}, use_global_device_ids=true | all-gather | bytes 270336 | tf_op jit(solution)/shard_map/while/body/eval_jaxpr/all_gather | solution.py:106
  191.9 19.5 %all-to-all-start.2 = ((bf16[8,4,1408]{2,1,0:T(4,128)(2,1)}), bf16[8,4,1408]{2,1,0:T(4,128)(2,1)S(1)}, u32[]{:S(2)}, u32[]{:S(2)}) async-start(bf16[8,4,1408]{2,1,0:T(4,128)(2,1)} %all_to_all.124), calls=%async_computation.2 | async-start | bytes 180224 | tf_op jit(solution)/shard_map/while/body/eval_jaxpr/all_to_all | solution.py:137
  215.5 6.5 %all-to-all-start.3 = ((bf16[8,4,1408]{2,1,0:T(4,128)(2,1)}), bf16[8,4,1408]{2,1,0:T(4,128)(2,1)S(1)}, u32[]{:S(2)}, u32[]{:S(2)}) async-start(bf16[8,4,1408]{2,1,0:T(4,128)(2,1)} %broadcast_select_fusion.2), calls=%async_computation.3 | async-start | bytes 180224 | tf_op jit(solution)/shard_map/while/body/eval_jaxpr/all_to_all | solution.py:140
  228.7 4.8 %all_gather.28 = bf16[64,1408]{1,0:T(8,128)(2,1)S(1)} all-gather(bf16[32,1408]{1,0:T(8,128)(2,1)S(1)} %divide_convert_fusion.11), channel_id=1, replica_groups=mesh['grp'=2,'sec'=8,'head'=2] {'head'}, dimensions={0}, use_global_device_ids=true | all-gather | bytes 270336 | tf_op jit(solution)/shard_map/while/body/eval_jaxpr/all_gather | solution.py:106
  243.8 25.6 %all-to-all-start.2 = ((bf16[8,4,1408]{2,1,0:T(4,128)(2,1)}), bf16[8,4,1408]{2,1,0:T(4,128)(2,1)S(1)}, u32[]{:S(2)}, u32[]{:S(2)}) async-start(bf16[8,4,1408]{2,1,0:T(4,128)(2,1)} %all_to_all.124), calls=%async_computation.2 | async-start | bytes 180224 | tf_op jit(solution)/shard_map/while/body/eval_jaxpr/all_to_all | solution.py:137
  273.5 6.5 %all-to-all-start.3 = ((bf16[8,4,1408]{2,1,0:T(4,128)(2,1)}), bf16[8,4,1408]{2,1,0:T(4,128)(2,1)S(1)}, u32[]{:S(2)}, u32[]{:S(2)}) async-start(bf16[8,4,1408]{2,1,0:T(4,128)(2,1)} %broadcast_select_fusion.2), calls=%async_computation.3 | async-start | bytes 180224 | tf_op jit(solution)/shard_map/while/body/eval_jaxpr/all_to_all | solution.py:140
  285.3 161.9 %while.47 = (s32[]{:T(128)}, bf16[32,1408]{1,0:T(8,128)(2,1)S(1)}, bf16[512,704]{0,1:T(8,128)(2,1)S(1)}, bf16[512,704]{0,1:T(8,128)(2,1)}, bf16[2,32,1408]{2,1,0...) while((s32[]{:T(128)}, bf16[32,1408]{1,0:T(8,128)(2,1)S(1)}, ...), condition=%wide.region_31.32_spmd.clone, body=%wide.region_16.31_spmd.clone.sunk | while | flops 856945728 | bytes 31071564 | solution.py:166
  286.6 4.8 %all_gather.27 = bf16[64,1408]{1,0:T(8,128)(2,1)S(1)} all-gather(bf16[32,1408]{1,0:T(8,128)(2,1)S(1)} %divide_convert_fusion.10), channel_id=1, replica_groups=mesh['grp'=2,'sec'=8,'head'=2] {'head'}, dimensions={0}, use_global_device_ids=true | all-gather | bytes 270336 | tf_op jit(solution)/shard_map/while/body/eval_jaxpr/all_gather | solution.py:106
  322.1 45.4 %collective-permute-done = bf16[32,1408]{1,0:T(8,128)(2,1)S(1)} collective-permute-done((bf16[32,1408]{1,0:T(8,128)(2,1)S(1)}, bf16[32,1408]{1,0:T(8,128)(2,1)S(1)}, u32[]{:S(2)}, u32[]{:S(2)}) %collective-permute-start) | collective-permute-done | bytes 90144 | tf_op jit(solution)/shard_map/while/body/eval_jaxpr/ppermute | solution.py:17
  368.4 5.3 %conditional.14 = (f32[32,1408]{1,0:T(8,128)S(1)}, f32[32]{0:T(128)S(1)}) conditional(s32[]{:T(128)} %convert_element_type.252, bf16[32,1408]{1,0:T(8,128)(2,1)S(1)} %bitcast_select_fusion.6, (bf16[2,32,1408]{2,1,0:T(8,128)(2,1)S(1)}, s32[]{:T(128)}, bf16[32,1408]{1,0:T(8,128)(2,1)S(1)}, bf16[2816,1408]{1,0:T(8,128)(2,1)}) %tuple.220), branch_computations={%region_17.18_spmd.clone, %region_19.22_spmd.clone} | conditional | flops 254521344 | bytes 9012500 | solution.py:104
  368.4 4.8 %fusion.66 = (f32[32]{0:T(128)S(1)}, f32[32,1408]{1,0:T(8,128)S(1)}) fusion(bf16[2816,1408]{1,0:T(8,128)(2,1)} %get-tuple-element.980, bf16[32,1408]{1,0:T(8,128)(2,1)S(1)} %dynamic-slice_bitcast_fusion.1, bf16[32,1408]{1,0:T(8,128)(2,1)S(1)} %get-tuple-element.977), kind=kOutput, calls=%fused_computation.145 | convolution fusion | flops 254160864 | bytes 8290432 | tf_op jit(solution)/shard_map/while/body/eval_jaxpr/cond/branch_1_fun/dot_general | solution.py:98
  377.7 16.6 %conditional.15 = (bf16[64,704]{1,0:T(8,128)(2,1)}, bf16[512,704]{0,1:T(8,128)(2,1)S(1)}, bf16[512,704]{0,1:T(8,128)(2,1)}) conditional(s32[]{:T(128)} %convert_element_type.253, (bf16[512,704]{0,1:T(8,128)(2,1)S(1)}, bf16[512,704]{0,1:T(8,128)(2,1)}) %tuple.221, (bf16[3,1408,704]{1,2,0:T(8,128)(2,1)}, bf16[64,1408]{1,0:T(8,128)(2,1)S(1)}, ...), branch_computations={%region_24.24_spmd, %region_25.30_spmd} | conditional | flops 475095904 | bytes 15372458 | solution.py:126
  408.7 5.3 %conditional.14 = (f32[32,1408]{1,0:T(8,128)S(1)}, f32[32]{0:T(128)S(1)}) conditional(s32[]{:T(128)} %convert_element_type.252, bf16[32,1408]{1,0:T(8,128)(2,1)S(1)} %bitcast_select_fusion.6, (bf16[2,32,1408]{2,1,0:T(8,128)(2,1)S(1)}, s32[]{:T(128)}, bf16[32,1408]{1,0:T(8,128)(2,1)S(1)}, bf16[2816,1408]{1,0:T(8,128)(2,1)}) %tuple.220), branch_computations={%region_17.18_spmd.clone, %region_19.22_spmd.clone} | conditional | flops 254521344 | bytes 9012500 | solution.py:104
  408.8 4.8 %fusion.66 = (f32[32]{0:T(128)S(1)}, f32[32,1408]{1,0:T(8,128)S(1)}) fusion(bf16[2816,1408]{1,0:T(8,128)(2,1)} %get-tuple-element.980, bf16[32,1408]{1,0:T(8,128)(2,1)S(1)} %dynamic-slice_bitcast_fusion.1, bf16[32,1408]{1,0:T(8,128)(2,1)S(1)} %get-tuple-element.977), kind=kOutput, calls=%fused_computation.145 | convolution fusion | flops 254160864 | bytes 8290432 | tf_op jit(solution)/shard_map/while/body/eval_jaxpr/cond/branch_1_fun/dot_general | solution.py:98
  418.3 15.3 %conditional.15 = (bf16[64,704]{1,0:T(8,128)(2,1)}, bf16[512,704]{0,1:T(8,128)(2,1)S(1)}, bf16[512,704]{0,1:T(8,128)(2,1)}) conditional(s32[]{:T(128)} %convert_element_type.253, (bf16[512,704]{0,1:T(8,128)(2,1)S(1)}, bf16[512,704]{0,1:T(8,128)(2,1)}) %tuple.221, (bf16[3,1408,704]{1,2,0:T(8,128)(2,1)}, bf16[64,1408]{1,0:T(8,128)(2,1)S(1)}, ...), branch_computations={%region_24.24_spmd, %region_25.30_spmd} | conditional | flops 475095904 | bytes 15372458 | solution.py:126
  (316 shorter events, 217.5 us)
Async XLA Ops:
  6.5 17.4 %all-gather.3.cloned.1.call-start = ((), (), s32[]{:S(2)}) async-start(), calls=%async_computation.4 | async-start | bytes 5947392 | tf_op jit(solution)/shard_map/all_gather | solution.py:85
  37.6 22.4 %all-to-all-start.2 = ((bf16[8,4,1408]{2,1,0:T(4,128)(2,1)}), bf16[8,4,1408]{2,1,0:T(4,128)(2,1)S(1)}, u32[]{:S(2)}, u32[]{:S(2)}) async-start(bf16[8,4,1408]{2,1,0:T(4,128)(2,1)} %all_to_all.124), calls=%async_computation.2 | async-start | bytes 180224 | tf_op jit(solution)/shard_map/while/body/eval_jaxpr/all_to_all | solution.py:137
  61.4 8.6 %all-to-all-start.3 = ((bf16[8,4,1408]{2,1,0:T(4,128)(2,1)}), bf16[8,4,1408]{2,1,0:T(4,128)(2,1)S(1)}, u32[]{:S(2)}, u32[]{:S(2)}) async-start(bf16[8,4,1408]{2,1,0:T(4,128)(2,1)} %broadcast_select_fusion.2), calls=%async_computation.3 | async-start | bytes 180224 | tf_op jit(solution)/shard_map/while/body/eval_jaxpr/all_to_all | solution.py:140
  67.3 5.3 %collective-permute-start.1 = (bf16[32,1408]{1,0:T(8,128)(2,1)S(1)}, bf16[32,1408]{1,0:T(8,128)(2,1)S(1)}, u32[]{:S(2)}, u32[]{:S(2)}) collective-permute-start(bf16[32,1408]{1,0:T(8,128)(2,1)S(1)} %get-tuple-element.1515), channel_id=1, source_target_pairs={{0,2},{2,4},{4,6},{6,8},{8,10},{10,12},{12,14},{1,3},{3,5},{5,7},{... | collective-permute-start | bytes 270344 | tf_op jit(solution)/shard_map/while/body/eval_jaxpr/ppermute | solution.py:17
  80.4 4.8 %all-to-all-start.1 = ((bf16[2,32,704]{2,1,0:T(8,128)(2,1)}), bf16[2,32,704]{2,1,0:T(8,128)(2,1)S(1)}, u32[]{:S(2)}, u32[]{:S(2)}) async-start(bf16[2,32,704]{2,1,0:T(8,128)(2,1)} %bitcast.114), calls=%async_computation.1 | async-start | bytes 196608 | tf_op jit(solution)/shard_map/while/body/eval_jaxpr/all_to_all | solution.py:129
  88.9 21.0 %all-to-all-start.2 = ((bf16[8,4,1408]{2,1,0:T(4,128)(2,1)}), bf16[8,4,1408]{2,1,0:T(4,128)(2,1)S(1)}, u32[]{:S(2)}, u32[]{:S(2)}) async-start(bf16[8,4,1408]{2,1,0:T(4,128)(2,1)} %all_to_all.124), calls=%async_computation.2 | async-start | bytes 180224 | tf_op jit(solution)/shard_map/while/body/eval_jaxpr/all_to_all | solution.py:137
  111.3 9.5 %all-to-all-start.3 = ((bf16[8,4,1408]{2,1,0:T(4,128)(2,1)}), bf16[8,4,1408]{2,1,0:T(4,128)(2,1)S(1)}, u32[]{:S(2)}, u32[]{:S(2)}) async-start(bf16[8,4,1408]{2,1,0:T(4,128)(2,1)} %broadcast_select_fusion.2), calls=%async_computation.3 | async-start | bytes 180224 | tf_op jit(solution)/shard_map/while/body/eval_jaxpr/all_to_all | solution.py:140
  118.1 5.3 %collective-permute-start.1 = (bf16[32,1408]{1,0:T(8,128)(2,1)S(1)}, bf16[32,1408]{1,0:T(8,128)(2,1)S(1)}, u32[]{:S(2)}, u32[]{:S(2)}) collective-permute-start(bf16[32,1408]{1,0:T(8,128)(2,1)S(1)} %get-tuple-element.1515), channel_id=1, source_target_pairs={{0,2},{2,4},{4,6},{6,8},{8,10},{10,12},{12,14},{1,3},{3,5},{5,7},{... | collective-permute-start | bytes 270344 | tf_op jit(solution)/shard_map/while/body/eval_jaxpr/ppermute | solution.py:17
  131.5 4.8 %all-to-all-start.1 = ((bf16[2,32,704]{2,1,0:T(8,128)(2,1)}), bf16[2,32,704]{2,1,0:T(8,128)(2,1)S(1)}, u32[]{:S(2)}, u32[]{:S(2)}) async-start(bf16[2,32,704]{2,1,0:T(8,128)(2,1)} %bitcast.114), calls=%async_computation.1 | async-start | bytes 196608 | tf_op jit(solution)/shard_map/while/body/eval_jaxpr/all_to_all | solution.py:129
  139.9 22.6 %all-to-all-start.2 = ((bf16[8,4,1408]{2,1,0:T(4,128)(2,1)}), bf16[8,4,1408]{2,1,0:T(4,128)(2,1)S(1)}, u32[]{:S(2)}, u32[]{:S(2)}) async-start(bf16[8,4,1408]{2,1,0:T(4,128)(2,1)} %all_to_all.124), calls=%async_computation.2 | async-start | bytes 180224 | tf_op jit(solution)/shard_map/while/body/eval_jaxpr/all_to_all | solution.py:137
  163.9 8.8 %all-to-all-start.3 = ((bf16[8,4,1408]{2,1,0:T(4,128)(2,1)}), bf16[8,4,1408]{2,1,0:T(4,128)(2,1)S(1)}, u32[]{:S(2)}, u32[]{:S(2)}) async-start(bf16[8,4,1408]{2,1,0:T(4,128)(2,1)} %broadcast_select_fusion.2), calls=%async_computation.3 | async-start | bytes 180224 | tf_op jit(solution)/shard_map/while/body/eval_jaxpr/all_to_all | solution.py:140
  170.1 5.3 %collective-permute-start.1 = (bf16[32,1408]{1,0:T(8,128)(2,1)S(1)}, bf16[32,1408]{1,0:T(8,128)(2,1)S(1)}, u32[]{:S(2)}, u32[]{:S(2)}) collective-permute-start(bf16[32,1408]{1,0:T(8,128)(2,1)S(1)} %get-tuple-element.1515), channel_id=1, source_target_pairs={{0,2},{2,4},{4,6},{6,8},{8,10},{10,12},{12,14},{1,3},{3,5},{5,7},{... | collective-permute-start | bytes 270344 | tf_op jit(solution)/shard_map/while/body/eval_jaxpr/ppermute | solution.py:17
  183.4 4.8 %all-to-all-start.1 = ((bf16[2,32,704]{2,1,0:T(8,128)(2,1)}), bf16[2,32,704]{2,1,0:T(8,128)(2,1)S(1)}, u32[]{:S(2)}, u32[]{:S(2)}) async-start(bf16[2,32,704]{2,1,0:T(8,128)(2,1)} %bitcast.114), calls=%async_computation.1 | async-start | bytes 196608 | tf_op jit(solution)/shard_map/while/body/eval_jaxpr/all_to_all | solution.py:129
  191.9 22.2 %all-to-all-start.2 = ((bf16[8,4,1408]{2,1,0:T(4,128)(2,1)}), bf16[8,4,1408]{2,1,0:T(4,128)(2,1)S(1)}, u32[]{:S(2)}, u32[]{:S(2)}) async-start(bf16[8,4,1408]{2,1,0:T(4,128)(2,1)} %all_to_all.124), calls=%async_computation.2 | async-start | bytes 180224 | tf_op jit(solution)/shard_map/while/body/eval_jaxpr/all_to_all | solution.py:137
  215.5 9.2 %all-to-all-start.3 = ((bf16[8,4,1408]{2,1,0:T(4,128)(2,1)}), bf16[8,4,1408]{2,1,0:T(4,128)(2,1)S(1)}, u32[]{:S(2)}, u32[]{:S(2)}) async-start(bf16[8,4,1408]{2,1,0:T(4,128)(2,1)} %broadcast_select_fusion.2), calls=%async_computation.3 | async-start | bytes 180224 | tf_op jit(solution)/shard_map/while/body/eval_jaxpr/all_to_all | solution.py:140
  222.0 5.3 %collective-permute-start.1 = (bf16[32,1408]{1,0:T(8,128)(2,1)S(1)}, bf16[32,1408]{1,0:T(8,128)(2,1)S(1)}, u32[]{:S(2)}, u32[]{:S(2)}) collective-permute-start(bf16[32,1408]{1,0:T(8,128)(2,1)S(1)} %get-tuple-element.1515), channel_id=1, source_target_pairs={{0,2},{2,4},{4,6},{6,8},{8,10},{10,12},{12,14},{1,3},{3,5},{5,7},{... | collective-permute-start | bytes 270344 | tf_op jit(solution)/shard_map/while/body/eval_jaxpr/ppermute | solution.py:17
  235.3 4.8 %all-to-all-start.1 = ((bf16[2,32,704]{2,1,0:T(8,128)(2,1)}), bf16[2,32,704]{2,1,0:T(8,128)(2,1)S(1)}, u32[]{:S(2)}, u32[]{:S(2)}) async-start(bf16[2,32,704]{2,1,0:T(8,128)(2,1)} %bitcast.114), calls=%async_computation.1 | async-start | bytes 196608 | tf_op jit(solution)/shard_map/while/body/eval_jaxpr/all_to_all | solution.py:129
  243.8 28.2 %all-to-all-start.2 = ((bf16[8,4,1408]{2,1,0:T(4,128)(2,1)}), bf16[8,4,1408]{2,1,0:T(4,128)(2,1)S(1)}, u32[]{:S(2)}, u32[]{:S(2)}) async-start(bf16[8,4,1408]{2,1,0:T(4,128)(2,1)} %all_to_all.124), calls=%async_computation.2 | async-start | bytes 180224 | tf_op jit(solution)/shard_map/while/body/eval_jaxpr/all_to_all | solution.py:137
  273.5 9.2 %all-to-all-start.3 = ((bf16[8,4,1408]{2,1,0:T(4,128)(2,1)}), bf16[8,4,1408]{2,1,0:T(4,128)(2,1)S(1)}, u32[]{:S(2)}, u32[]{:S(2)}) async-start(bf16[8,4,1408]{2,1,0:T(4,128)(2,1)} %broadcast_select_fusion.2), calls=%async_computation.3 | async-start | bytes 180224 | tf_op jit(solution)/shard_map/while/body/eval_jaxpr/all_to_all | solution.py:140
  280.0 5.3 %collective-permute-start.1 = (bf16[32,1408]{1,0:T(8,128)(2,1)S(1)}, bf16[32,1408]{1,0:T(8,128)(2,1)S(1)}, u32[]{:S(2)}, u32[]{:S(2)}) collective-permute-start(bf16[32,1408]{1,0:T(8,128)(2,1)S(1)} %get-tuple-element.1515), channel_id=1, source_target_pairs={{0,2},{2,4},{4,6},{6,8},{8,10},{10,12},{12,14},{1,3},{3,5},{5,7},{... | collective-permute-start | bytes 270344 | tf_op jit(solution)/shard_map/while/body/eval_jaxpr/ppermute | solution.py:17
  301.2 5.7 %collective-permute-start = (bf16[32,1408]{1,0:T(8,128)(2,1)S(1)}, bf16[32,1408]{1,0:T(8,128)(2,1)S(1)}, u32[]{:S(2)}, u32[]{:S(2)}) collective-permute-start(bf16[32,1408]{1,0:T(8,128)(2,1)S(1)} %get-tuple-element.1491), channel_id=1, source_target_pairs={{0,2},{2,4},{4,6},{6,8},{8,10},{10,12},{12,14},{1,3},{3,5},{5,7},{... | collective-permute-start | bytes 270344 | tf_op jit(solution)/shard_map/while/body/eval_jaxpr/ppermute | solution.py:17
  320.8 46.7 %collective-permute-start = (bf16[32,1408]{1,0:T(8,128)(2,1)S(1)}, bf16[32,1408]{1,0:T(8,128)(2,1)S(1)}, u32[]{:S(2)}, u32[]{:S(2)}) collective-permute-start(bf16[32,1408]{1,0:T(8,128)(2,1)S(1)} %get-tuple-element.1491), channel_id=1, source_target_pairs={{0,2},{2,4},{4,6},{6,8},{8,10},{10,12},{12,14},{1,3},{3,5},{5,7},{... | collective-permute-start | bytes 270344 | tf_op jit(solution)/shard_map/while/body/eval_jaxpr/ppermute | solution.py:17
  402.0 5.7 %collective-permute-start = (bf16[32,1408]{1,0:T(8,128)(2,1)S(1)}, bf16[32,1408]{1,0:T(8,128)(2,1)S(1)}, u32[]{:S(2)}, u32[]{:S(2)}) collective-permute-start(bf16[32,1408]{1,0:T(8,128)(2,1)S(1)} %get-tuple-element.1491), channel_id=1, source_target_pairs={{0,2},{2,4},{4,6},{6,8},{8,10},{10,12},{12,14},{1,3},{3,5},{5,7},{... | collective-permute-start | bytes 270344 | tf_op jit(solution)/shard_map/while/body/eval_jaxpr/ppermute | solution.py:17
  441.4 5.7 %collective-permute-start = (bf16[32,1408]{1,0:T(8,128)(2,1)S(1)}, bf16[32,1408]{1,0:T(8,128)(2,1)S(1)}, u32[]{:S(2)}, u32[]{:S(2)}) collective-permute-start(bf16[32,1408]{1,0:T(8,128)(2,1)S(1)} %get-tuple-element.1491), channel_id=1, source_target_pairs={{0,2},{2,4},{4,6},{6,8},{8,10},{10,12},{12,14},{1,3},{3,5},{5,7},{... | collective-permute-start | bytes 270344 | tf_op jit(solution)/shard_map/while/body/eval_jaxpr/ppermute | solution.py:17
  (15 other events, 72.5 us)
Sparse Core Ops, SparseCore 0:
  8.9 14.9 all-gather.2
where the time goes:
time: 459 us; the launch traced here: 455 us
  starting transfers between devices  179 us (39%)
  waiting for transfers between devices  116 us (25%)
  matrix products  47.7 us (10%)
  local copies, waits for them, and re-layouts  36.6 us (8%)
  blocking collectives  33.5 us (7%)
  other arithmetic  21 us (5%)
  between operations  14.1 us (3%)
  loops' own time  7.32 us (2%)
    all_to_all x5, starting transfers between devices, run_segment(): lax.all_to_all(produced, 'sec', split_axis=0, concat_axis=0, tiled=True)  102 us
    ppermute x9, waiting for transfers between devices, shifted(): lax.ppermute(value, axis, [(source, source + steps) for source in range(l...  71.4 us
    all_gather x9, blocking collectives, run_segment(): rows_all = lax.all_gather(normed, 'head', axis=0, tiled=True)  33.5 us
    all_to_all x9, starting transfers between devices, run_segment(): lax.all_to_all(attended, 'head', split_axis=0, concat_axis=1, tiled=True)  33 us
    all_to_all x5, starting transfers between devices, run_segment(): lax.all_to_all(chosen, 'sec', split_axis=0, concat_axis=0, tiled=True)  32 us
    dot_general x9, matrix products, run_segment(): update = jnp.dot(regrouped, w_out, preferred_element_type=jnp.float32)  25.2 us
    all_to_all x5, waiting for transfers between devices, run_segment(): lax.all_to_all(produced, 'sec', split_axis=0, concat_axis=0, tiled=True)  14 us
    all_gather x1, waiting for transfers between devices, body(): w_out = lax.all_gather(out_weight[0], 'head', axis=0, tiled=True)  13.1 us
  transfers between devices with their start and end apart: 29, of which 29 were waited for; matrix products, arithmetic and copies ran while one was open for 1% of the time, Pallas kernels for 0%

commit v1 on v0

v1 whole, which is shorter than its diff:
```python
import functools
import math

import jax
import jax.numpy as jnp
import numpy as np
from jax import lax
from jax.experimental import pallas as pl
from jax.experimental.pallas import tpu as pltpu
from jax.sharding import PartitionSpec as P

HEAD_DIM = 88
EPSILON = 1e-06
LANES = 128
MESH = pl.DeviceIdType.MESH


def layer_norm(x):
    centred = x - jnp.mean(x, axis=-1, keepdims=True)
    variance = jnp.mean(centred * centred, axis=-1, keepdims=True)
    return centred * lax.rsqrt(variance + EPSILON)


def column_chunks(width, count):
    tiles = width // LANES
    step = -(-tiles // count)
    step += step % 2
    edges = list(range(0, tiles, step)) + [tiles]
    return [(a * LANES, (b - a) * LANES) for a, b in zip(edges[:-1], edges[1:])]


def kernel(
    dims,
    order_ref, tile_ref, patches_ref, gain_ref, freq_ref, kv_hbm, wqkv_hbm, wout_hbm, wskip_hbm,
    out_ref,
    wqkv, wout, wskip, kbuf, vbuf, ubuf, sbuf, pre, hsb, qs, ks, att, pbuf, psend, precv, obuf, cosb, sinb, gains,
    w_sem, kv_sem, wo_sem, ws_sem,
    u_send, u_recv, r_send, r_recv, s_send, s_recv, t_send, t_recv, p_send, p_recv,
):
    sections, patch_count, own_rows, width, lanes, tile_rows, chunks = dims
    rows = own_rows * 2
    heads = lanes // HEAD_DIM
    wide = qs.shape[1]
    half = sections // 2
    last = sections - 1
    sec = lax.axis_index("sec")
    core = lax.axis_index("head")
    peer = 1 - core
    partner = last - sec
    own = pl.ds(pl.multiple_of(core * own_rows, own_rows), own_rows)
    other = pl.ds(pl.multiple_of(peer * own_rows, own_rows), own_rows)
    far_partner = (sec < half - 1) | (sec > half)

    w_copies = [pltpu.make_async_copy(wqkv_hbm.at[0, c], wqkv.at[c], w_sem.at[c]) for c in range(3)]
    k_copy = pltpu.make_async_copy(kv_hbm.at[0, 0], kbuf.at[pl.ds(0, tile_rows)], kv_sem.at[0])
    v_copy = pltpu.make_async_copy(kv_hbm.at[0, 1], vbuf.at[pl.ds(0, tile_rows)], kv_sem.at[1])
    o_copy = pltpu.make_async_copy(wout_hbm.at[0], wout, wo_sem)
    top_copy = pltpu.make_async_copy(wskip_hbm.at[0, pl.ds(0, width)], wskip.at[pl.ds(0, width)], ws_sem.at[0])
    low_copy = pltpu.make_async_copy(wskip_hbm.at[0, pl.ds(width, width)], wskip.at[pl.ds(width, width)], ws_sem.at[1])
    for copy in (*w_copies, k_copy, v_copy, o_copy):
        copy.start()

    @pl.when(sec >= half)
    def _():
        low_copy.start()
        top_copy.start()

    barrier = pltpu.get_barrier_semaphore()
    pl.semaphore_signal(barrier, inc=1, device_id={"head": peer}, device_id_type=MESH)

    @pl.when(sec < last)
    def _():
        pl.semaphore_signal(barrier, inc=1, device_id={"sec": sec + 1}, device_id_type=MESH)

    @pl.when(sec > 0)
    def _():
        pl.semaphore_signal(barrier, inc=1, device_id={"sec": sec - 1}, device_id_type=MESH)

    @pl.when(far_partner)
    def _():
        pl.semaphore_signal(barrier, inc=1, device_id={"sec": partner}, device_id_type=MESH)

    greeted = (
        1
        + jnp.where(sec < last, 1, 0)
        + jnp.where(sec > 0, 1, 0)
        + jnp.where(far_partner, 1, 0)
    )
    pl.semaphore_wait(barrier, greeted)

    def relay_u(k, j):
        start, size = chunks[j]
        piece = ubuf.at[k, own, pl.ds(start, size)]
        return pltpu.make_async_remote_copy(
            piece, piece, r_send.at[k, j], r_recv.at[k, j], device_id={"head": peer}, device_id_type=MESH
        )

    def send_u(k, j):
        start, size = chunks[j]
        return pltpu.make_async_remote_copy(
            obuf.at[k, :, pl.ds(start, size)],
            ubuf.at[k, own, pl.ds(start, size)],
            u_send.at[k, j],
            u_recv.at[k, j],
            device_id={"sec": jnp.minimum(sec + 1, last)},
            device_id_type=MESH,
        )

    def send_skip(k):
        return pltpu.make_async_remote_copy(
            obuf.at[k], sbuf.at[k, own], s_send.at[k], s_recv.at[k], device_id={"sec": partner}, device_id_type=MESH
        )

    def relay_skip(k):
        piece = sbuf.at[k, own]
        return pltpu.make_async_remote_copy(
            piece, piece, t_send.at[k], t_recv.at[k], device_id={"head": peer}, device_id_type=MESH
        )

    def send_part(k, j):
        start, size = chunks[j]
        return pltpu.make_async_remote_copy(
            psend.at[k, :, pl.ds(start, size)],
            precv.at[k, :, pl.ds(start, size)],
            p_send.at[k, j],
            p_recv.at[k, j],
            device_id={"head": peer},
            device_id_type=MESH,
        )

    @pl.when(sec == 0)
    def _():
        for k in range(patch_count):
            ubuf[k, own, :] = patches_ref[k]

    tiles = [(t, min(LANES, lanes - t)) for t in range(0, lanes, LANES)]
    lane = [lax.broadcasted_iota(jnp.int32, (1, LANES), 1) + t for t, _ in tiles]

    def spans(h):
        return [t for t in range(len(tiles)) if t * LANES < (h + 1) * HEAD_DIM and (t + 1) * LANES > h * HEAD_DIM]

    def mask(h, t):
        return (lane[t] >= h * HEAD_DIM) & (lane[t] < (h + 1) * HEAD_DIM)

    def tables(k, _):
        start = tile_ref[0] * tile_rows + order_ref[k] * rows
        position = (lax.broadcasted_iota(jnp.int32, (rows, LANES), 0) + start).astype(jnp.float32)
        for t in range(len(tiles)):
            cols = pl.ds(t * LANES, LANES)
            angle = position * freq_ref[0:1, cols]
            cosb[k, :, cols] = jnp.cos(angle)
            sinb[k, :, cols] = jnp.sin(angle) * freq_ref[1:2, cols]
        return 0

    lax.fori_loop(0, patch_count, tables, 0)
    qs[...] = jnp.zeros_like(qs)
    ks[...] = jnp.zeros_like(ks)
    gains[...] = jnp.zeros_like(gains)
    gains[:, pl.ds(0, lanes)] = gain_ref[0].astype(jnp.float32)
    kbuf[pl.ds(tile_rows, rows * patch_count), :] = jnp.zeros((rows * patch_count, lanes), jnp.bfloat16)
    vbuf[pl.ds(tile_rows, rows * patch_count), :] = jnp.zeros((rows * patch_count, lanes), jnp.bfloat16)

    @pl.when(sec >= half)
    def _():
        low_copy.wait()

    @pl.when(sec > half)
    def _():
        def ahead(k, _):
            relay = relay_skip(k)
            send_skip(k).wait_recv()
            relay.start()
            relay.wait_recv()
            pre[k] = jnp.dot(sbuf[k], wskip[pl.ds(width, width), :], preferred_element_type=jnp.float32)
            return 0

        lax.fori_loop(0, patch_count, ahead, 0)

    @pl.when(sec >= half)
    def _():
        top_copy.wait()

    def head_sums(parts):
        sums = [None] * heads
        for h in range(heads):
            total = None
            for t in spans(h):
                term = jnp.where(mask(h, t), parts[t], 0.0)
                total = term if total is None else total + term
            sums[h] = jnp.sum(total, axis=1, keepdims=True) * (1.0 / HEAD_DIM)
        result = []
        for t in range(len(tiles)):
            value = jnp.zeros((rows, LANES), jnp.float32)
            for h in range(heads):
                if t in spans(h):
                    value = jnp.where(mask(h, t), sums[h], value)
            result.append(value)
        return result

    def head_norm(buf, which, k):
        parts = [buf[:, pl.ds(t * LANES, LANES)] for t in range(len(tiles))]
        means = head_sums(parts)
        parts = [a - m for a, m in zip(parts, means)]
        variances = head_sums([a * a for a in parts])
        for t in range(len(tiles)):
            cols = pl.ds(t * LANES, LANES)
            buf[:, cols] = parts[t] * lax.rsqrt(variances[t] + EPSILON) * gains[which : which + 1, cols]
        value = buf[...]
        ahead = pltpu.roll(value, wide - HEAD_DIM // 2, 1)
        behind = pltpu.roll(value, HEAD_DIM // 2, 1)
        turned = jnp.where(freq_ref[1:2, :] < 0.0, ahead, behind)
        return value * cosb[k] + turned * sinb[k]

    def step(k, _):
        for j in range(len(chunks)):
            @pl.when(sec > 0)
            def _():
                send_u(k, j).wait_recv()

            relay_u(k, j).start()
        for j in range(len(chunks)):
            relay_u(k, j).wait_recv()

        @pl.when(sec < half)
        def _():
            hsb[...] = ubuf[k]

        @pl.when(sec == half)
        def _():
            pre[k] = jnp.dot(ubuf[k], wskip[pl.ds(width, width), :], preferred_element_type=jnp.float32)

        @pl.when(sec >= half)
        def _():
            mixed = pre[k] + jnp.dot(ubuf[k], wskip[pl.ds(0, width), :], preferred_element_type=jnp.float32)
            hsb[...] = layer_norm(mixed).astype(jnp.bfloat16)

        normed = layer_norm(hsb[...].astype(jnp.float32)).astype(jnp.bfloat16)

        @pl.when(k == 0)
        def _():
            for copy in (*w_copies, k_copy, v_copy, o_copy):
                copy.wait()

        qs[:, pl.ds(0, lanes)] = jnp.dot(normed, wqkv[0], preferred_element_type=jnp.float32)
        ks[:, pl.ds(0, lanes)] = jnp.dot(normed, wqkv[1], preferred_element_type=jnp.float32)
        fresh = pl.ds(pl.multiple_of(tile_rows + k * rows, rows), rows)
        vbuf[fresh, :] = jnp.dot(normed, wqkv[2], preferred_element_type=jnp.float32).astype(jnp.bfloat16)
        q_rot = head_norm(qs, 0, k)
        k_rot = head_norm(ks, 1, k)
        kbuf[fresh, :] = k_rot[:, :lanes].astype(jnp.bfloat16)

        keys = tile_rows + patch_count * rows
        column = lax.broadcasted_iota(jnp.int32, (1, keys), 1)
        slot = column // rows
        stale_slots = tile_rows // rows
        gone = slot > stale_slots + k
        for i in range(patch_count):
            gone = gone | ((slot == order_ref[i]) & (i <= k))
        keep = jnp.where(gone, 0.0, 1.0)
        scale = math.log2(math.e) / math.sqrt(HEAD_DIM)
        mixed_tiles = [None] * len(tiles)
        for h in range(heads):
            found = spans(h)
            low = found[0] * LANES
            span = min(lanes, (found[-1] + 1) * LANES) - low
            query = jnp.concatenate(
                [jnp.where(mask(h, t), q_rot[:, t * LANES : (t + 1) * LANES], 0.0) for t in found], axis=1
            )[:, :span].astype(jnp.bfloat16)
            window = pl.ds(low, span)
            scores = lax.dot_general(
                query, kbuf[:, window], (((1,), (1,)), ((), ())), preferred_element_type=jnp.float32
            )
            expd = jnp.exp2(scores * scale) * keep
            inverse = 1.0 / jnp.sum(expd, axis=1, keepdims=True)
            mixed = jnp.dot(expd.astype(jnp.bfloat16), vbuf[:, window], preferred_element_type=jnp.float32) * inverse
            for t in found:
                size = tiles[t][1]
                value = mixed[:, t * LANES - low : t * LANES - low + size]
                before = mixed_tiles[t]
                mixed_tiles[t] = value if before is None else jnp.where(mask(h, t)[:, :size], value, before)
        for t, (begin, size) in enumerate(tiles):
            att[:, pl.ds(begin, size)] = mixed_tiles[t].astype(jnp.bfloat16)

        for j, (begin, size) in enumerate(chunks):
            cols = pl.ds(begin, size)
            pbuf[:, cols] = jnp.dot(att[...], wout[:, cols], preferred_element_type=jnp.float32)
            psend[k, :, cols] = pbuf[other, cols].astype(jnp.bfloat16)
            send_part(k, j).start()
        for j, (begin, size) in enumerate(chunks):
            cols = pl.ds(begin, size)
            mine = hsb[own, cols].astype(jnp.float32) + pbuf[own, cols]
            send_part(k, j).wait_recv()
            produced = (mine + precv[k, :, cols].astype(jnp.float32)).astype(jnp.bfloat16)
            obuf[k, :, cols] = produced

            @pl.when(sec < last)
            def _():
                send_u(k, j).start()

            out_ref[0, k, :, cols] = produced

        @pl.when(sec < half - 1)
        def _():
            send_skip(k).start()

        return 0

    lax.fori_loop(0, patch_count, step, 0)

    def finish(k, _):
        for j in range(len(chunks)):
            relay_u(k, j).wait_send()
            send_part(k, j).wait_send()

            @pl.when(sec < last)
            def _():
                send_u(k, j).wait_send()

        @pl.when(sec < half - 1)
        def _():
            send_skip(k).wait_send()

        @pl.when(sec > half)
        def _():
            relay_skip(k).wait_send()

        return 0

    lax.fori_loop(0, patch_count, finish, 0)


def body(patches, stale_kv, qkv_weight, out_weight, skip_joined_weight, qk_gain, order, tile_index):
    patch_count, own_rows, width = patches.shape
    sections = lax.axis_size("sec")
    tile_rows, lanes = stale_kv.shape[2:]
    rows = own_rows * 2
    wide = -(-lanes // LANES) * LANES
    chunks = column_chunks(width, 2)
    keys = tile_rows + patch_count * rows
    half_width = HEAD_DIM // 2
    index = np.arange(wide) % HEAD_DIM
    inverse = 10000.0 ** (-(index % half_width).astype(np.float64) / half_width)
    sign = np.where(index < half_width, -1.0, 1.0)
    freq = jnp.asarray(np.stack([inverse, sign]).astype(np.float32))
    count = len(chunks)
    bf, f32 = jnp.bfloat16, jnp.float32
    vmem = pl.BlockSpec(memory_space=pltpu.VMEM)
    smem = pl.BlockSpec(memory_space=pltpu.SMEM)
    hbm = pl.BlockSpec(memory_space=pl.ANY)
    dma = pltpu.SemaphoreType.DMA
    dims = (sections, patch_count, own_rows, width, lanes, tile_rows, chunks)
    return pl.pallas_call(
        functools.partial(kernel, dims),
        out_shape=jax.ShapeDtypeStruct((1, patch_count, own_rows, width), bf),
        in_specs=[smem, smem, vmem, vmem, vmem, hbm, hbm, hbm, hbm],
        out_specs=vmem,
        scratch_shapes=[
            pltpu.VMEM((3, width, lanes), bf),
            pltpu.VMEM((lanes, width), bf),
            pltpu.VMEM((2 * width, width), bf),
            pltpu.VMEM((keys, lanes), bf),
            pltpu.VMEM((keys, lanes), bf),
            pltpu.VMEM((patch_count, rows, width), bf),
            pltpu.VMEM((patch_count, rows, width), bf),
            pltpu.VMEM((patch_count, rows, width), f32),
            pltpu.VMEM((rows, width), bf),
            pltpu.VMEM((rows, wide), f32),
            pltpu.VMEM((rows, wide), f32),
            pltpu.VMEM((rows, lanes), bf),
            pltpu.VMEM((rows, width), f32),
            pltpu.VMEM((patch_count, own_rows, width), bf),
            pltpu.VMEM((patch_count, own_rows, width), bf),
            pltpu.VMEM((patch_count, own_rows, width), bf),
            pltpu.VMEM((patch_count, rows, wide), f32),
            pltpu.VMEM((patch_count, rows, wide), f32),
            pltpu.VMEM((2, wide), f32),
            dma((3,)),
            dma((2,)),
            dma,
            dma((2,)),
            dma((patch_count, count)),
            dma((patch_count, count)),
            dma((patch_count, count)),
            dma((patch_count, count)),
            dma((patch_count,)),
            dma((patch_count,)),
            dma((patch_count,)),
            dma((patch_count,)),
            dma((patch_count, count)),
            dma((patch_count, count)),
        ],
        compiler_params=pltpu.CompilerParams(
            collective_id=0, has_side_effects=True, vmem_limit_bytes=44 * 1024 * 1024
        ),
    )(order, tile_index, patches, qk_gain, freq, stale_kv, qkv_weight, out_weight, skip_joined_weight)


def solution(mesh):
    return jax.shard_map(
        body,
        mesh=mesh,
        in_specs=(
            P("grp", "head", None),
            P(("grp", "sec"), None, None, "head"),
            P("sec", None, None, "head"),
            P("sec", "head", None),
            P("sec", None, None),
            P("sec", None, "head"),
            P("grp"),
            P("grp"),
        ),
        out_specs=P("sec", "grp", "head", None),
        check_vma=False,
    )
```

time: 459 us -> 108 us (0.24)
  starting transfers between devices: 179 us -> 0 us
  waiting for transfers between devices: 116 us -> 0 us
  Pallas kernels: 0 us -> 89.8 us
  matrix products: 47.7 us -> 0 us
  blocking collectives: 33.5 us -> 0 us
  other arithmetic: 21 us -> 0 us
  local copies, waits for them, and re-layouts: 36.6 us -> 17.4 us
  between operations: 14.1 us -> 0.68 us
  loops' own time: 7.32 us -> 0 us
    all_to_all x19 -> x0, starting transfers between devices: 167 us -> none  [the longest x5 102 us: run_segment(): lax.all_to_all(produced, 'sec', split_axis=0, concat_axis=0, tiled=True)]
    pallas_call x0 -> x1, Pallas kernels: none -> 89.8 us  [body(): pl.pallas_call(functools.partial(kernel, dims), out_shape=jax.ShapeDtypeS...]
    ppermute x9 -> x0, waiting for transfers between devices: 71.4 us -> none  [shifted(): lax.ppermute(value, axis, [(source, source + steps) for source in range(l...]
    dot_general x17 -> x0, matrix products: 47.7 us -> none  [the longest x9 25.2 us: run_segment(): update = jnp.dot(regrouped, w_out, preferred_element_type=jnp.float32)]
    all_gather x9 -> x0, blocking collectives: 33.5 us -> none  [run_segment(): rows_all = lax.all_gather(normed, 'head', axis=0, tiled=True)]
    all_to_all x19 -> x0, waiting for transfers between devices: 30.5 us -> none  [the longest x5 14 us: run_segment(): lax.all_to_all(produced, 'sec', split_axis=0, concat_axis=0, tiled=True)]
    unnamed x2 -> x15, local copies, waits for them, and re-layouts: 0.67 us -> 17.4 us
    all_gather x1 -> x0, waiting for transfers between devices: 13.1 us -> none  [body(): w_out = lax.all_gather(out_weight[0], 'head', axis=0, tiled=True)]
  transfers between devices with their start and end apart: 29 -> 0, of which waited for: 29 -> 0; matrix products, arithmetic and copies ran while one was open for 1% -> 0% of each run, Pallas kernels for 0% -> 0%
where the time goes in v1:
time: 108 us
  Pallas kernels  89.8 us (83%)
  local copies, waits for them, and re-layouts  17.4 us (16%)
    pallas_call x1, Pallas kernels, body(): pl.pallas_call(functools.partial(kernel, dims), out_shape=jax.ShapeDtypeS...  89.8 us
    unnamed x15, local copies, waits for them, and re-layouts  17.4 us

profile of v1, /device:TPU:29, one launch (start us, length us, event | category | flops | bytes accessed | tf_op | source)
XLA Modules:
  0.0 107.9 jit_solution(11292980737892746257)
XLA Ops:
  0.7 1.7 %copy.10.kv_hbm = bf16[1,2,512,704]{3,2,1,0:T(8,128)(2,1)S(1)} copy(bf16[1,2,512,704]{2,3,1,0:T(8,128)(2,1)} %param.10) | data formatting | bytes 2883584 | tf_op args[1]
  2.4 0.0 copy-start.1
  2.4 9.2 %copy.11.wqkv_hbm = bf16[1,3,1408,704]{3,2,1,0:T(8,128)(2,1)} copy(bf16[1,3,1408,704]{2,3,1,0:T(8,128)(2,1)} %param.11) | data formatting | bytes 11894784 | tf_op args[2]
  11.6 0.0 copy-done.1
  11.6 0.0 copy-start
  11.6 2.8 %copy-done = bf16[1,3,1408,704]{3,2,1,0:T(8,128)(2,1)S(1)} copy-done((bf16[1,3,1408,704]{3,2,1,0:T(8,128)(2,1)S(1)}, bf16[1,3,1408,704]{3,2,1,0:T(8,128)(2,1)}, u32[]{:S(2)}) %copy-start) | copy-done | bytes 5947416
  14.4 0.0 copy-start.2
  14.4 0.9 copy-done.2
  15.3 0.0 copy-start.3
  15.3 0.7 copy-done.3
  16.0 0.0 copy-start.4
  16.0 0.7 copy-done.4
  16.7 0.0 copy-start.5
  16.7 0.7 copy-done.5
  17.4 89.8 %shard_map.91 = bf16[1,2,32,1408]{3,2,1,0:T(8,128)(2,1)S(1)} custom-call(s32[8]{0:T(128)S(1)} %copy-done.5, s32[1]{0:T(128)S(6)} %copy.13.tile_ref, bf16[2,32,1408]{2,1,0:T(8,128)(2,1)S(1)} %copy-done.2, bf16[1,2,704]{2,1,0:T(2,128)(2,1)S(1)} %copy-done.4, f32[2,768]{1,0:T(2,128)S(1)} %copy-done.3, bf16[1,2,512,704]{3,2,1,0:T(8,128)(2,1)S(1)} %copy.10.kv_hbm, ...), custom_call_target="tpu_custom_call" | custom-call | tf_op jit(solution)/shard_map/pallas_call | solution.py:352
  107.2 0.7 copy.14
Async XLA Ops:
  2.4 9.2 %copy-start.1 = (bf16[1,704,1408]{2,1,0:T(8,128)(2,1)S(1)}, bf16[1,704,1408]{2,1,0:T(8,128)(2,1)}, u32[]{:S(2)}) copy-start(bf16[1,704,1408]{2,1,0:T(8,128)(2,1)} %wout_hbm.1) | copy-start | bytes 5947396
  11.6 2.8 %copy-start = (bf16[1,3,1408,704]{3,2,1,0:T(8,128)(2,1)S(1)}, bf16[1,3,1408,704]{3,2,1,0:T(8,128)(2,1)}, u32[]{:S(2)}) copy-start(bf16[1,3,1408,704]{3,2,1,0:T(8,128)(2,1)} %copy.11.wqkv_hbm) | copy-start | bytes 17842180
  14.4 0.9 copy-start.2
  15.3 0.7 copy-start.3
  16.0 0.7 copy-start.4
  16.7 0.7 copy-start.5

commit v2 on v1

--- a/solution.py
+++ b/solution.py
@@ -21,6 +21,10 @@
     return centred * lax.rsqrt(variance + EPSILON)
 
 
+def across(a, b):
+    return lax.dot_general(a, b, (((1,), (1,)), ((), ())), preferred_element_type=jnp.float32)
+
+
 def column_chunks(width, count):
     tiles = width // LANES
     step = -(-tiles // count)
@@ -31,10 +35,10 @@
 
 def kernel(
     dims,
-    order_ref, tile_ref, patches_ref, gain_ref, freq_ref, kv_hbm, wqkv_hbm, wout_hbm, wskip_hbm,
+    order_ref, tile_ref, patches_hbm, gain_hbm, freq_hbm, kv_hbm, wqkv_hbm, wout_hbm, wskip_hbm,
     out_ref,
-    wqkv, wout, wskip, kbuf, vbuf, ubuf, sbuf, pre, hsb, qs, ks, att, pbuf, psend, precv, obuf, cosb, sinb, gains,
-    w_sem, kv_sem, wo_sem, ws_sem,
+    patches_ref, gain_ref, freq_ref, wqkv, wout, wskip, kbuf, vbuf, knew, vnew, ubuf, sbuf, pre, hsb, qs, ks, att, pbuf, psend, precv, obuf, cosb, sinb, gains,
+    in_sem, w_sem, kv_sem, wo_sem, ws_sem,
     u_send, u_recv, r_send, r_recv, s_send, s_recv, t_send, t_recv, p_send, p_recv,
 ):
     sections, patch_count, own_rows, width, lanes, tile_rows, chunks = dims
@@ -52,12 +56,17 @@
     far_partner = (sec < half - 1) | (sec > half)
 
     w_copies = [pltpu.make_async_copy(wqkv_hbm.at[0, c], wqkv.at[c], w_sem.at[c]) for c in range(3)]
-    k_copy = pltpu.make_async_copy(kv_hbm.at[0, 0], kbuf.at[pl.ds(0, tile_rows)], kv_sem.at[0])
-    v_copy = pltpu.make_async_copy(kv_hbm.at[0, 1], vbuf.at[pl.ds(0, tile_rows)], kv_sem.at[1])
+    k_copy = pltpu.make_async_copy(kv_hbm.at[0, 0], kbuf, kv_sem.at[0])
+    v_copy = pltpu.make_async_copy(kv_hbm.at[0, 1], vbuf, kv_sem.at[1])
     o_copy = pltpu.make_async_copy(wout_hbm.at[0], wout, wo_sem)
     top_copy = pltpu.make_async_copy(wskip_hbm.at[0, pl.ds(0, width)], wskip.at[pl.ds(0, width)], ws_sem.at[0])
     low_copy = pltpu.make_async_copy(wskip_hbm.at[0, pl.ds(width, width)], wskip.at[pl.ds(width, width)], ws_sem.at[1])
-    for copy in (*w_copies, k_copy, v_copy, o_copy):
+    small = [
+        pltpu.make_async_copy(patches_hbm, patches_ref, in_sem.at[0]),
+        pltpu.make_async_copy(freq_hbm, freq_ref, in_sem.at[1]),
+        pltpu.make_async_copy(gain_hbm, gain_ref, in_sem.at[2]),
+    ]
+    for copy in (*small, *w_copies, k_copy, v_copy, o_copy):
         copy.start()
 
     @pl.when(sec >= half)
@@ -128,6 +137,9 @@
             device_id_type=MESH,
         )
 
+    for copy in small:
+        copy.wait()
+
     @pl.when(sec == 0)
     def _():
         for k in range(patch_count):
@@ -157,8 +169,8 @@
     ks[...] = jnp.zeros_like(ks)
     gains[...] = jnp.zeros_like(gains)
     gains[:, pl.ds(0, lanes)] = gain_ref[0].astype(jnp.float32)
-    kbuf[pl.ds(tile_rows, rows * patch_count), :] = jnp.zeros((rows * patch_count, lanes), jnp.bfloat16)
-    vbuf[pl.ds(tile_rows, rows * patch_count), :] = jnp.zeros((rows * patch_count, lanes), jnp.bfloat16)
+    knew[...] = jnp.zeros_like(knew)
+    vnew[...] = jnp.zeros_like(vnew)
 
     @pl.when(sec >= half)
     def _():
@@ -241,22 +253,21 @@
             for copy in (*w_copies, k_copy, v_copy, o_copy):
                 copy.wait()
 
-        qs[:, pl.ds(0, lanes)] = jnp.dot(normed, wqkv[0], preferred_element_type=jnp.float32)
-        ks[:, pl.ds(0, lanes)] = jnp.dot(normed, wqkv[1], preferred_element_type=jnp.float32)
-        fresh = pl.ds(pl.multiple_of(tile_rows + k * rows, rows), rows)
-        vbuf[fresh, :] = jnp.dot(normed, wqkv[2], preferred_element_type=jnp.float32).astype(jnp.bfloat16)
+        qs[:, pl.ds(0, lanes)] = across(normed, wqkv[0])
+        ks[:, pl.ds(0, lanes)] = across(normed, wqkv[1])
+        fresh = pl.ds(pl.multiple_of(k * rows, rows), rows)
+        vnew[fresh, :] = across(normed, wqkv[2]).astype(jnp.bfloat16)
         q_rot = head_norm(qs, 0, k)
         k_rot = head_norm(ks, 1, k)
-        kbuf[fresh, :] = k_rot[:, :lanes].astype(jnp.bfloat16)
-
-        keys = tile_rows + patch_count * rows
-        column = lax.broadcasted_iota(jnp.int32, (1, keys), 1)
-        slot = column // rows
-        stale_slots = tile_rows // rows
-        gone = slot > stale_slots + k
+        knew[fresh, :] = k_rot[:, :lanes].astype(jnp.bfloat16)
+
+        slot = lax.broadcasted_iota(jnp.int32, (1, tile_rows), 1) // rows
+        gone = slot < 0
         for i in range(patch_count):
             gone = gone | ((slot == order_ref[i]) & (i <= k))
         keep = jnp.where(gone, 0.0, 1.0)
+        source = lax.broadcasted_iota(jnp.int32, (1, patch_count * rows), 1) // rows
+        keep_new = jnp.where(source > k, 0.0, 1.0)
         scale = math.log2(math.e) / math.sqrt(HEAD_DIM)
         mixed_tiles = [None] * len(tiles)
         for h in range(heads):
@@ -267,12 +278,15 @@
                 [jnp.where(mask(h, t), q_rot[:, t * LANES : (t + 1) * LANES], 0.0) for t in found], axis=1
             )[:, :span].astype(jnp.bfloat16)
             window = pl.ds(low, span)
-            scores = lax.dot_general(
-                query, kbuf[:, window], (((1,), (1,)), ((), ())), preferred_element_type=jnp.float32
+            scores = jnp.dot(query, kbuf[window, :], preferred_element_type=jnp.float32)
+            scores_new = across(query, knew[:, window])
+            expd = jnp.exp2(scores * scale) * keep
+            expd_new = jnp.exp2(scores_new * scale) * keep_new
+            total = jnp.sum(expd, axis=1, keepdims=True) + jnp.sum(expd_new, axis=1, keepdims=True)
+            mixed = across(expd.astype(jnp.bfloat16), vbuf[window, :]) + jnp.dot(
+                expd_new.astype(jnp.bfloat16), vnew[:, window], preferred_element_type=jnp.float32
             )
-            expd = jnp.exp2(scores * scale) * keep
-            inverse = 1.0 / jnp.sum(expd, axis=1, keepdims=True)
-            mixed = jnp.dot(expd.astype(jnp.bfloat16), vbuf[:, window], preferred_element_type=jnp.float32) * inverse
+            mixed = mixed * (1.0 / total)
             for t in found:
                 size = tiles[t][1]
                 value = mixed[:, t * LANES - low : t * LANES - low + size]
@@ -336,7 +350,6 @@
     rows = own_rows * 2
     wide = -(-lanes // LANES) * LANES
     chunks = column_chunks(width, 2)
-    keys = tile_rows + patch_count * rows
     half_width = HEAD_DIM // 2
     index = np.arange(wide) % HEAD_DIM
     inverse = 10000.0 ** (-(index % half_width).astype(np.float64) / half_width)
@@ -352,14 +365,19 @@
     return pl.pallas_call(
         functools.partial(kernel, dims),
         out_shape=jax.ShapeDtypeStruct((1, patch_count, own_rows, width), bf),
-        in_specs=[smem, smem, vmem, vmem, vmem, hbm, hbm, hbm, hbm],
+        in_specs=[smem, smem, hbm, hbm, hbm, hbm, hbm, hbm, hbm],
         out_specs=vmem,
         scratch_shapes=[
-            pltpu.VMEM((3, width, lanes), bf),
+            pltpu.VMEM(patches.shape, bf),
+            pltpu.VMEM(qk_gain.shape, bf),
+            pltpu.VMEM(freq.shape, f32),
+            pltpu.VMEM((3, lanes, width), bf),
             pltpu.VMEM((lanes, width), bf),
             pltpu.VMEM((2 * width, width), bf),
-            pltpu.VMEM((keys, lanes), bf),
-            pltpu.VMEM((keys, lanes), bf),
+            pltpu.VMEM((lanes, tile_rows), bf),
+            pltpu.VMEM((lanes, tile_rows), bf),
+            pltpu.VMEM((patch_count * rows, lanes), bf),
+            pltpu.VMEM((patch_count * rows, lanes), bf),
             pltpu.VMEM((patch_count, rows, width), bf),
             pltpu.VMEM((patch_count, rows, width), bf),
             pltpu.VMEM((patch_count, rows, width), f32),
@@ -375,6 +393,7 @@
             pltpu.VMEM((patch_count, rows, wide), f32),
             pltpu.VMEM((2, wide), f32),
             dma((3,)),
+            dma((3,)),
             dma((2,)),
             dma,
             dma((2,)),
@@ -390,9 +409,9 @@
             dma((patch_count, count)),
         ],
         compiler_params=pltpu.CompilerParams(
-            collective_id=0, has_side_effects=True, vmem_limit_bytes=44 * 1024 * 1024
+            collective_id=0, has_side_effects=True, vmem_limit_bytes=60 * 1024 * 1024
         ),
-    )(order, tile_index, patches, qk_gain, freq, stale_kv, qkv_weight, out_weight, skip_joined_weight)
+    )(order, tile_index, patches, qk_gain, freq, jnp.swapaxes(stale_kv, 2, 3), jnp.swapaxes(qkv_weight, 2, 3), out_weight, skip_joined_weight)
 
 
 def solution(mesh):

time: 108 us -> 96.5 us (0.89)
  local copies, waits for them, and re-layouts: 17.4 us -> 1.61 us
  Pallas kernels: 89.8 us -> 94 us
    unnamed x15 -> x1, local copies, waits for them, and re-layouts: 17.4 us -> 1.61 us
    pallas_call x1, Pallas kernels: 89.8 us -> 94 us  [body(): pl.pallas_call(functools.partial(kernel, dims), out_shape=jax.ShapeDtypeS...]
where the time goes in v2:
time: 96.5 us; the launch traced here: 96.3 us
  Pallas kernels  94 us (97%)
  local copies, waits for them, and re-layouts  1.61 us (2%)
    pallas_call x1, Pallas kernels, body(): pl.pallas_call(functools.partial(kernel, dims), out_shape=jax.ShapeDtypeS...  94 us

profile of v2, /device:TPU:29, one launch (start us, length us, event | category | flops | bytes accessed | tf_op | source)
XLA Modules:
  0.0 96.3 jit_solution(15007465874907392518)
XLA Ops:
  0.7 94.0 %shard_map.91 = bf16[1,2,32,1408]{3,2,1,0:T(8,128)(2,1)} custom-call(s32[8]{0:T(128)} %order_ref.1, s32[1]{0:T(128)S(6)} %copy.11.tile_ref, bf16[2,32,1408]{2,1,0:T(8,128)(2,1)} %patches_hbm.1, bf16[1,2,704]{2,1,0:T(2,128)(2,1)} %gain_hbm.1, f32[2,768]{1,0:T(2,128)} %constant.2.clone.freq_hbm, bf16[1,2,704,512]{3,2,1,0:T(8,128)(2,1)} %bitcast.3, ...), custom_call_target="tpu_custom_call" | custom-call | tf_op jit(solution)/shard_map/pallas_call | solution.py:365
  94.7 1.6 %copy.12 = bf16[1,2,32,1408]{3,2,1,0:T(8,128)(2,1)} copy(bf16[1,2,32,1408]{3,2,1,0:T(8,128)(2,1)} %shard_map.91) | data formatting | bytes 360448

commit v3 on v2

--- a/solution.py
+++ b/solution.py
@@ -176,6 +176,10 @@
     def _():
         low_copy.wait()
 
+    @pl.when(sec == half)
+    def _():
+        pre[...] = jnp.zeros_like(pre)
+
     @pl.when(sec > half)
     def _():
         def ahead(k, _):
@@ -230,21 +234,25 @@
                 send_u(k, j).wait_recv()
 
             relay_u(k, j).start()
-        for j in range(len(chunks)):
+        for j, (begin, size) in enumerate(chunks):
             relay_u(k, j).wait_recv()
+            cols = pl.ds(begin, size)
+
+            @pl.when(sec == half)
+            def _():
+                pre[k] += jnp.dot(ubuf[k, :, cols], wskip[pl.ds(width + begin, size), :], preferred_element_type=jnp.float32)
+
+            @pl.when(sec >= half)
+            def _():
+                pre[k] += jnp.dot(ubuf[k, :, cols], wskip[cols, :], preferred_element_type=jnp.float32)
 
         @pl.when(sec < half)
         def _():
             hsb[...] = ubuf[k]
 
-        @pl.when(sec == half)
-        def _():
-            pre[k] = jnp.dot(ubuf[k], wskip[pl.ds(width, width), :], preferred_element_type=jnp.float32)
-
         @pl.when(sec >= half)
         def _():
-            mixed = pre[k] + jnp.dot(ubuf[k], wskip[pl.ds(0, width), :], preferred_element_type=jnp.float32)
-            hsb[...] = layer_norm(mixed).astype(jnp.bfloat16)
+            hsb[...] = layer_norm(pre[k]).astype(jnp.bfloat16)
 
         normed = layer_norm(hsb[...].astype(jnp.float32)).astype(jnp.bfloat16)
 
@@ -265,10 +273,11 @@
         gone = slot < 0
         for i in range(patch_count):
             gone = gone | ((slot == order_ref[i]) & (i <= k))
-        keep = jnp.where(gone, 0.0, 1.0)
+        keep = jnp.where(gone, -1e30, 0.0)
         source = lax.broadcasted_iota(jnp.int32, (1, patch_count * rows), 1) // rows
-        keep_new = jnp.where(source > k, 0.0, 1.0)
+        keep_new = jnp.where(source > k, -1e30, 0.0)
         scale = math.log2(math.e) / math.sqrt(HEAD_DIM)
+        q_rot = q_rot * scale
         mixed_tiles = [None] * len(tiles)
         for h in range(heads):
             found = spans(h)
@@ -280,8 +289,8 @@
             window = pl.ds(low, span)
             scores = jnp.dot(query, kbuf[window, :], preferred_element_type=jnp.float32)
             scores_new = across(query, knew[:, window])
-            expd = jnp.exp2(scores * scale) * keep
-            expd_new = jnp.exp2(scores_new * scale) * keep_new
+            expd = jnp.exp2(scores + keep)
+            expd_new = jnp.exp2(scores_new + keep_new)
             total = jnp.sum(expd, axis=1, keepdims=True) + jnp.sum(expd_new, axis=1, keepdims=True)
             mixed = across(expd.astype(jnp.bfloat16), vbuf[window, :]) + jnp.dot(
                 expd_new.astype(jnp.bfloat16), vnew[:, window], preferred_element_type=jnp.float32

time: 96.5 us -> 96 us (level)
  no operation moved by 1% of the time
where the time goes in v3:
time: 96 us; the launch traced here: 95.8 us
  Pallas kernels  93.6 us (98%)
  local copies, waits for them, and re-layouts  1.61 us (2%)
    pallas_call x1, Pallas kernels, body(): pl.pallas_call(functools.partial(kernel, dims), out_shape=jax.ShapeDtypeS...  93.6 us

profile of v3, /device:TPU:29, one launch (start us, length us, event | category | flops | bytes accessed | tf_op | source)
XLA Modules:
  0.0 95.8 jit_solution(15216696092771029432)
XLA Ops:
  0.7 93.6 %shard_map.91 = bf16[1,2,32,1408]{3,2,1,0:T(8,128)(2,1)} custom-call(s32[8]{0:T(128)} %order_ref.1, s32[1]{0:T(128)S(6)} %copy.11.tile_ref, bf16[2,32,1408]{2,1,0:T(8,128)(2,1)} %patches_hbm.1, bf16[1,2,704]{2,1,0:T(2,128)(2,1)} %gain_hbm.1, f32[2,768]{1,0:T(2,128)} %constant.2.clone.freq_hbm, bf16[1,2,704,512]{3,2,1,0:T(8,128)(2,1)} %bitcast.3, ...), custom_call_target="tpu_custom_call" | custom-call | tf_op jit(solution)/shard_map/pallas_call | solution.py:374
  94.2 1.6 %copy.12 = bf16[1,2,32,1408]{3,2,1,0:T(8,128)(2,1)} copy(bf16[1,2,32,1408]{3,2,1,0:T(8,128)(2,1)} %shard_map.91) | data formatting | bytes 360448
